TPU v7x, 32 devices: a whole 2x2x4 slice. The times are simulated.
32 devices in a mesh: dp: 4 (over z), ctx: 8 (over y, x, core).
Axes of the slice: x: 2, y: 2, z: 4, core: 2. Of those that a mesh axis runs over, the one named last changes fastest.
Arguments:
- hidden_in: bfloat16 [4, 1024, 768], P('dp', 'ctx'), may hold values from -6 to 6
- segment_ids: int32 [4, 1024], P('dp', 'ctx'), may hold values from 0 to 4, as said below
- w_qkv: bfloat16 [768, 2304], P('dp'), may hold values from -0.21875 to 0.21875
- w_out: bfloat16 [768, 768], P('dp'), may hold values from -4 to 4
- w_in: bfloat16 [768, 2304], P('dp'), may hold values from -0.21875 to 0.21875
- w_down: bfloat16 [1152, 768], P('dp'), may hold values from -0.1875 to 0.1875
- gain_attn: bfloat16 [768], P('dp'), may hold values from 0.5 to 1.5
- gain_mlp: bfloat16 [768], P('dp'), may hold values from 0.5 to 1.5
- cotangent: bfloat16 [4, 1024, 768], P('dp', 'ctx'), may hold values from -6 to 6
Outputs:
- output: bfloat16 [4, 1024, 768], P('dp', 'ctx')
- grad_input: float32 [4, 1024, 768], P('dp', 'ctx')
- grad_qkv: float32 [768, 2304], P('dp')
- grad_out: float32 [768, 768], P('dp')
- grad_in: float32 [768, 2304], P('dp')
- grad_down: float32 [1152, 768], P('dp')
- grad_gain_attn: float32 [768], P('dp')
- grad_gain_mlp: float32 [768], P('dp')
Inputs may be any that keep to these rules, and one draw needn't show every extreme that they name: `segment_ids`: ids never fall along a sequence; each sequence holds documents 0 to 4; document 2 begins within the first 128 tokens and ends within the last 128; every other document is shorter than 128 tokens.
All inputs are finite; a program needn't handle non-finite values.
Results may differ from a plain program's by a relative error of at most 0.024.
Values may be sent and summed in bfloat16 or wider, within the bound.
A program may use at most 256 MiB of HBM per device.

v0:
```python
import jax
import jax.numpy as jnp
from jax import lax
from jax.sharding import PartitionSpec as P

HEADS = 12
EPSILON = 1e-05
ROPE_THETA = 160000.0
NEGATIVE = -1e30


def layer_norm(values, gain_row):
    average = jnp.mean(values, axis=-1, keepdims=True)
    centred = values - average
    spread = jnp.mean(centred * centred, axis=-1, keepdims=True)
    return centred * lax.rsqrt(spread + EPSILON) * gain_row


def rope_tables(first_row, row_count, head_size):
    position = (first_row + jnp.arange(row_count, dtype=jnp.int32)).astype(jnp.float32)
    frequency = ROPE_THETA ** (-jnp.arange(0, head_size, 2, dtype=jnp.float32) / head_size)
    angles = position[:, None] * frequency[None, :]
    angles = jnp.concatenate([angles, angles], axis=-1)
    return (jnp.cos(angles)[:, None, :], jnp.sin(angles)[:, None, :])


def rotary(values, cosines, sines):
    half_size = values.shape[-1] // 2
    turned = jnp.concatenate([-values[..., half_size:], values[..., :half_size]], axis=-1)
    return values * cosines + turned * sines


def rotary_back(grads, cosines, sines):
    half_size = grads.shape[-1] // 2
    shifted = grads * sines
    return grads * cosines + jnp.concatenate(
        [shifted[..., half_size:], -shifted[..., :half_size]], axis=-1
    )


def geglu(gate_in, gate_up):
    return jax.nn.gelu(gate_in, approximate=False) * gate_up


def contract_rows(left_side, right_side):
    return lax.dot_general(
        left_side, right_side, (((0,), (0,)), ((), ())), preferred_element_type=jnp.float32
    )


def contract_cols(left_side, right_side):
    return lax.dot_general(
        left_side, right_side, (((1,), (1,)), ((), ())), preferred_element_type=jnp.float32
    )


def local(hidden_in, segment_ids, w_qkv, w_out, w_in, w_down, gain_attn, gain_mlp, cotangent):
    local_rows = hidden_in.shape[1]
    model_width = hidden_in.shape[2]
    head_count = HEADS
    head_size = model_width // head_count
    score_scale = head_size ** (-0.5)
    head_shape = (local_rows, head_count, head_size)
    shards = (w_qkv, w_out, w_in, w_down, gain_attn, gain_mlp)
    qkv_full, out_full, in_full, down_full, attn_scale, mlp_scale = (
        lax.all_gather(shards[0], "dp", axis=0, tiled=True),
        lax.all_gather(shards[1], "dp", axis=0, tiled=True),
        lax.all_gather(shards[2], "dp", axis=0, tiled=True),
        lax.all_gather(shards[3], "dp", axis=0, tiled=True),
        lax.all_gather(shards[4], "dp", axis=0, tiled=True),
        lax.all_gather(shards[5], "dp", axis=0, tiled=True),
    )
    hidden_units = in_full.shape[1] // 2
    source = hidden_in[0].astype(jnp.float32)
    own_ids = segment_ids[0]
    cosines, sines = rope_tables(lax.axis_index("ctx") * local_rows, local_rows, head_size)
    normed_one = layer_norm(source, attn_scale.astype(jnp.float32)).astype(jnp.bfloat16)
    projected = jnp.dot(normed_one, qkv_full, preferred_element_type=jnp.float32)
    queries = rotary(projected[:, :model_width].reshape(head_shape), cosines, sines).astype(
        jnp.bfloat16
    )
    own_keys = rotary(
        projected[:, model_width : 2 * model_width].reshape(head_shape), cosines, sines
    ).astype(jnp.bfloat16)
    value_flat = projected[:, 2 * model_width :].astype(jnp.bfloat16)
    own_values = value_flat.reshape(head_shape)
    key_flat = own_keys.reshape(local_rows, model_width)
    query_flat = queries.reshape(local_rows, model_width)
    highest = jnp.full((head_count, local_rows), NEGATIVE, jnp.float32)
    block_keys = lax.all_gather(key_flat, "ctx", axis=0, tiled=True)
    block_values = lax.all_gather(value_flat, "ctx", axis=0, tiled=True)
    block_ids = lax.all_gather(own_ids, "ctx", axis=0, tiled=True)
    piece_rows = block_keys.shape[0]
    scores = (
        jnp.einsum(
            "qhe,khe->hqk",
            queries,
            block_keys.reshape(piece_rows, head_count, head_size),
            preferred_element_type=jnp.float32,
        )
        * score_scale
    )
    allowed = (own_ids[:, None] == block_ids[None, :])[None]
    scores = jnp.where(allowed, scores, NEGATIVE)
    raised = jnp.maximum(highest, jnp.max(scores, axis=-1))
    weights = jnp.where(allowed, jnp.exp(scores - raised[..., None]), 0.0)
    row_total = jnp.sum(weights, axis=-1)
    update = jnp.einsum(
        "hqk,khe->qhe",
        weights.astype(jnp.bfloat16),
        block_values.reshape(piece_rows, head_count, head_size),
        preferred_element_type=jnp.float32,
    )
    summed = update
    highest, row_total, summed = (raised, row_total, summed)
    attention = summed / jnp.transpose(row_total)[:, :, None]
    log_total = highest + jnp.log(row_total)
    attended = attention.reshape(local_rows, model_width).astype(jnp.bfloat16)
    middle = source + jnp.dot(attended, out_full, preferred_element_type=jnp.float32)
    normed_two = layer_norm(middle, mlp_scale.astype(jnp.float32)).astype(jnp.bfloat16)
    lifted = jnp.dot(normed_two, in_full, preferred_element_type=jnp.float32)
    gate_in = lifted[:, :hidden_units]
    gate_up = lifted[:, hidden_units:]
    mixed_units = geglu(gate_in, gate_up).astype(jnp.bfloat16)
    result = (middle + jnp.dot(mixed_units, down_full, preferred_element_type=jnp.float32)).astype(
        jnp.bfloat16
    )
    qkv_back, out_back, in_back, down_back, attn_back, mlp_back = (
        lax.all_gather(shards[0], "dp", axis=0, tiled=True),
        lax.all_gather(shards[1], "dp", axis=0, tiled=True),
        lax.all_gather(shards[2], "dp", axis=0, tiled=True),
        lax.all_gather(shards[3], "dp", axis=0, tiled=True),
        lax.all_gather(shards[4], "dp", axis=0, tiled=True),
        lax.all_gather(shards[5], "dp", axis=0, tiled=True),
    )
    upstream = cotangent[0]
    grad_down = contract_rows(mixed_units, upstream)
    grad_mixed = contract_cols(upstream, down_back)
    _, pull_gate = jax.vjp(geglu, gate_in, gate_up)
    grad_gate_in, grad_gate_up = pull_gate(grad_mixed)
    grad_lifted = jnp.concatenate([grad_gate_in, grad_gate_up], axis=1).astype(jnp.bfloat16)
    grad_in = contract_rows(normed_two, grad_lifted)
    grad_normed_two = contract_cols(grad_lifted, in_back)
    _, pull_two = jax.vjp(layer_norm, middle, mlp_back.astype(jnp.float32))
    grad_middle_part, grad_mlp_gain = pull_two(grad_normed_two)
    grad_middle = upstream.astype(jnp.float32) + grad_middle_part
    grad_branch = grad_middle.astype(jnp.bfloat16)
    grad_out = contract_rows(attended, grad_branch)
    grad_attended = contract_cols(grad_branch, out_back).astype(jnp.bfloat16)
    grad_heads = grad_attended.reshape(head_shape)
    products = jnp.transpose(jnp.sum(grad_heads.astype(jnp.float32) * attention, axis=-1))
    all_log, all_products, all_ids = (
        lax.all_gather(log_total, "ctx", axis=1, tiled=True),
        lax.all_gather(products, "ctx", axis=1, tiled=True),
        lax.all_gather(own_ids, "ctx", axis=0, tiled=True),
    )
    block_keys = lax.all_gather(key_flat, "ctx", axis=0, tiled=True)
    block_values = lax.all_gather(value_flat, "ctx", axis=0, tiled=True)
    block_ids = lax.all_gather(own_ids, "ctx", axis=0, tiled=True)
    piece_rows = block_keys.shape[0]
    key_heads = block_keys.reshape(piece_rows, head_count, head_size)
    scores = (
        jnp.einsum("qhe,khe->hqk", queries, key_heads, preferred_element_type=jnp.float32)
        * score_scale
    )
    allowed = (own_ids[:, None] == block_ids[None, :])[None]
    probabilities = jnp.where(allowed, jnp.exp(scores - log_total[..., None]), 0.0)
    grad_probs = jnp.einsum(
        "qhe,khe->hqk",
        grad_heads,
        block_values.reshape(piece_rows, head_count, head_size),
        preferred_element_type=jnp.float32,
    )
    grad_scores = (probabilities * (grad_probs - products[..., None])).astype(jnp.bfloat16)
    grad_queries = score_scale * jnp.einsum(
        "hqk,khe->qhe", grad_scores, key_heads, preferred_element_type=jnp.float32
    )
    block_queries = lax.all_gather(query_flat, "ctx", axis=0, tiled=True)
    block_grads = lax.all_gather(grad_attended, "ctx", axis=0, tiled=True)
    piece_rows = block_queries.shape[0]
    query_heads = block_queries.reshape(piece_rows, head_count, head_size)
    grad_rows = block_grads.reshape(piece_rows, head_count, head_size)
    scores = (
        jnp.einsum("qhe,khe->hqk", query_heads, own_keys, preferred_element_type=jnp.float32)
        * score_scale
    )
    allowed = (all_ids[:, None] == own_ids[None, :])[None]
    probabilities = jnp.where(allowed, jnp.exp(scores - all_log[..., None]), 0.0)
    grad_values = jnp.einsum(
        "hqk,qhe->khe",
        probabilities.astype(jnp.bfloat16),
        grad_rows,
        preferred_element_type=jnp.float32,
    )
    grad_probs = jnp.einsum(
        "qhe,khe->hqk", grad_rows, own_values, preferred_element_type=jnp.float32
    )
    grad_scores = (probabilities * (grad_probs - all_products[..., None])).astype(jnp.bfloat16)
    grad_keys = score_scale * jnp.einsum(
        "hqk,qhe->khe", grad_scores, query_heads, preferred_element_type=jnp.float32
    )
    grad_keys, grad_values = (grad_keys, grad_values)
    grad_projected = jnp.concatenate(
        [
            rotary_back(grad_queries, cosines, sines).reshape(local_rows, model_width),
            rotary_back(grad_keys, cosines, sines).reshape(local_rows, model_width),
            grad_values.reshape(local_rows, model_width),
        ],
        axis=1,
    ).astype(jnp.bfloat16)
    grad_qkv = contract_rows(normed_one, grad_projected)
    grad_normed_one = contract_cols(grad_projected, qkv_back)
    _, pull_one = jax.vjp(layer_norm, source, attn_back.astype(jnp.float32))
    grad_source, grad_attn_gain = pull_one(grad_normed_one)
    grad_input = grad_middle + grad_source
    local_grads = (grad_qkv, grad_out, grad_in, grad_down, grad_attn_gain, grad_mlp_gain)
    shares = (
        lax.psum_scatter(
            local_grads[0].astype(jnp.bfloat16), "dp", scatter_dimension=0, tiled=True
        ).astype(jnp.float32),
        lax.psum_scatter(
            local_grads[1].astype(jnp.bfloat16), "dp", scatter_dimension=0, tiled=True
        ).astype(jnp.float32),
        lax.psum_scatter(
            local_grads[2].astype(jnp.bfloat16), "dp", scatter_dimension=0, tiled=True
        ).astype(jnp.float32),
        lax.psum_scatter(
            local_grads[3].astype(jnp.bfloat16), "dp", scatter_dimension=0, tiled=True
        ).astype(jnp.float32),
        lax.psum_scatter(
            local_grads[4].astype(jnp.bfloat16), "dp", scatter_dimension=0, tiled=True
        ).astype(jnp.float32),
        lax.psum_scatter(
            local_grads[5].astype(jnp.bfloat16), "dp", scatter_dimension=0, tiled=True
        ).astype(jnp.float32),
    )
    shares = (
        lax.psum(shares[0].astype(jnp.bfloat16), "ctx").astype(jnp.float32),
        lax.psum(shares[1].astype(jnp.bfloat16), "ctx").astype(jnp.float32),
        lax.psum(shares[2].astype(jnp.bfloat16), "ctx").astype(jnp.float32),
        lax.psum(shares[3].astype(jnp.bfloat16), "ctx").astype(jnp.float32),
        lax.psum(shares[4].astype(jnp.bfloat16), "ctx").astype(jnp.float32),
        lax.psum(shares[5].astype(jnp.bfloat16), "ctx").astype(jnp.float32),
    )
    return (
        result[None],
        grad_input[None],
        shares[0],
        shares[1],
        shares[2],
        shares[3],
        shares[4],
        shares[5],
    )


def solution(mesh):
    in_specs = (
        P("dp", "ctx", None),
        P("dp", "ctx"),
        P("dp", None),
        P("dp", None),
        P("dp", None),
        P("dp", None),
        P("dp"),
        P("dp"),
        P("dp", "ctx", None),
    )
    out_specs = (
        P("dp", "ctx", None),
        P("dp", "ctx", None),
        P("dp", None),
        P("dp", None),
        P("dp", None),
        P("dp", None),
        P("dp"),
        P("dp"),
    )
    return jax.shard_map(local, mesh=mesh, in_specs=in_specs, out_specs=out_specs, check_vma=False)
```

profile of v0, /device:TPU:0, one launch (start us, length us, event | category | flops | bytes accessed | tf_op | source)
XLA Modules:
  0.0 630.1 jit_solution(16062213591360769307)
XLA Ops:
  8.0 1.3 fusion.87
  11.6 13.6 %all-reduce.7 = (bf16[768]{0:T(1024)(128)(2,1)S(1)}, bf16[768]{0:T(1024)(128)(2,1)S(1)}) all-reduce(bf16[768]{0:T(1024)(128)(2,1)S(1)} %dynamic-update-slice, bf16[768]{0:T(1024)(128)(2,1)S(1)} %dynamic-update-slice.1), channel_id=1, replica_groups=mesh['dp'=4,'ctx'=8] {'dp'}, use_global_device_ids=true, to_apply=%add | all-reduce | flops 1536 | bytes 6144
  28.5 53.9 %all-gather.10.cloned.1.call-done = bf16[768,2304]{1,0:T(8,128)(2,1)} async-done(((bf16[192,2304]{1,0:T(8,128)(2,1)}), bf16[768,2304]{1,0:T(8,128)(2,1)}) %all-gather.10.cloned.1.call-update) | async-done | bytes 3538960 | tf_op jit(solution)/shard_map/all_gather | solution.py:66
  82.3 2.8 fusion.78
  87.6 2.0 add_convert_fusion.2
  92.2 8.7 %all-gather = s32[1,1024]{1,0:T(1,128)S(1)} all-gather(s32[1,128]{1,0:T(1,128)S(1)} %copy-done.44), channel_id=2, replica_groups=mesh['dp'=4,'ctx'=8] {'ctx'}, dimensions={1}, use_global_device_ids=true | all-gather | bytes 4608 | tf_op jit(solution)/shard_map/all_gather | solution.py:92
  101.1 12.9 %all-gather.14.cloned.1.call-done = bf16[1024,768]{1,0:T(8,128)(2,1)} async-done(((bf16[128,768]{1,0:T(8,128)(2,1)}), bf16[1024,768]{1,0:T(8,128)(2,1)}) %all-gather.14.cloned.1.call-update) | async-done | bytes 1572880 | tf_op jit(solution)/shard_map/all_gather | solution.py:90
  114.0 1.7 copy.50
  115.7 1.3 select_reduce_fusion
  117.1 2.7 copy-done
  119.7 2.0 fusion.1
  121.7 19.9 %all-gather.12.cloned.1.call-done = bf16[1024,768]{1,0:T(8,128)(2,1)} async-done(((bf16[128,768]{1,0:T(8,128)(2,1)}), bf16[1024,768]{1,0:T(8,128)(2,1)}) %all-gather.12.cloned.1.call-update) | async-done | bytes 1572880 | tf_op jit(solution)/shard_map/all_gather | solution.py:91
  141.6 2.6 copy.45
  144.2 5.8 fusion.88
  150.0 23.5 %all-gather.16.cloned.1.call-done = bf16[768,768]{1,0:T(8,128)(2,1)} async-done(((bf16[192,768]{1,0:T(8,128)(2,1)}), bf16[768,768]{1,0:T(8,128)(2,1)}) %all-gather.16.cloned.1.call-update) | async-done | bytes 1179664 | tf_op jit(solution)/shard_map/all_gather | solution.py:67
  173.5 1.7 fusion.89
  176.0 68.1 %all-gather.18.cloned.1.call-done = bf16[768,2304]{1,0:T(8,128)(2,1)} async-done(((bf16[192,2304]{1,0:T(8,128)(2,1)}), bf16[768,2304]{1,0:T(8,128)(2,1)}) %all-gather.18.cloned.1.call-update) | async-done | bytes 3538960 | tf_op jit(solution)/shard_map/all_gather | solution.py:68
  244.1 2.7 fusion.81
  246.8 37.7 %all-gather.20.cloned.1.call-done = bf16[1152,768]{1,0:T(8,128)(2,1)} async-done(((bf16[288,768]{1,0:T(8,128)(2,1)}), bf16[1152,768]{1,0:T(8,128)(2,1)}) %all-gather.20.cloned.1.call-update) | async-done | bytes 1769488 | tf_op jit(solution)/shard_map/all_gather | solution.py:69
  284.5 3.3 add_convert_fusion
  288.7 1.9 multiply_reduce_fusion
  291.0 1.2 convolution_convert_fusion.4
  292.5 2.4 convolution_convert_fusion.3
  295.0 1.9 convolution_convert_fusion.2
  297.0 3.9 convolution_convert_fusion
  301.0 1.6 broadcast_compare_fusion
  304.5 7.0 %all-gather.22.cloned.1.call-done = bf16[1024,768]{1,0:T(8,128)(2,1)} async-done(((bf16[128,768]{1,0:T(8,128)(2,1)}), bf16[1024,768]{1,0:T(8,128)(2,1)}) %all-gather.22.cloned.1.call-update) | async-done | bytes 1572880 | tf_op jit(solution)/shard_map/all_gather | solution.py:178
  311.5 2.6 copy.54
  314.8 10.1 %all_gather.59 = f32[12,1024]{1,0:T(8,128)} all-gather(f32[12,128]{1,0:T(8,128)S(1)} %log_add_fusion), channel_id=1, replica_groups=mesh['dp'=4,'ctx'=8] {'ctx'}, dimensions={1}, use_global_device_ids=true | all-gather | bytes 55296 | tf_op jit(solution)/shard_map/all_gather | solution.py:153
  326.0 9.1 %all_gather.61 = f32[12,1024]{1,0:T(8,128)} all-gather(f32[12,128]{1,0:T(8,128)S(1)} %bitcast.131), channel_id=1, replica_groups=mesh['dp'=4,'ctx'=8] {'ctx'}, dimensions={1}, use_global_device_ids=true | all-gather | bytes 55296 | tf_op jit(solution)/shard_map/all_gather | solution.py:154
  335.0 5.2 fusion.54
  340.3 2.7 copy.55
  343.0 9.0 %fusion.17 = f32[128,12,64]{0,2,1:T(8,128)} fusion(bf16[1024,12,64]{0,2,1:T(8,128)(2,1)} %bitcast.105, f32[12,1024,128]{2,1,0:T(8,128)} %fusion.54, f32[12,1024]{1,0:T(8,128)S(1)} %copy-done.30, f32[12,1024]{1,0:T(8,128)S(1)} %copy-done.28, pred[1024,128]{1,0:T(8,128)(4,1)S(1)} %copy-done.26, bf16[1024,12,64]{0,2,1:T(8,128)(2,1)} %bitcast.114, ...), kind=kOutput, calls=%fused_computation.22 | convolution fusion | flops 412090368 | bytes 10256384 | tf_op jit(solution)/shard_map/hqk,qhe->khe/dot_general | solution.py:199
  352.0 7.1 %broadcast_multiply_fusion.1 = (f32[128,12,64]{0,2,1:T(8,128)}, f32[128,12,64]{0,2,1:T(8,128)S(1)}, f32[128,12,64]{0,2,1:T(8,128)}) fusion(f32[128,64]{0,1:T(8,128)} %get-tuple-element.47, f32[128,12,64]{0,2,1:T(8,128)} %fusion.17, bf16[1024,12,64]{0,2,1:T(8,128)(2,1)S(1)} %bitcast.103, f32[12,128,1024]{2,1,0:T(8,128)} %copy-done, ...), kind=kOutput, calls=%fused_computation.102 | convolution fusion | flops 412286976 | bytes 11382784 | tf_op jit(solution)/shard_map/hqk,khe->qhe/dot_general | solution.py:175
  359.1 1.2 fusion.85
  360.3 1.3 fusion.48
  361.6 5.0 fusion.23
  367.3 3.0 convolution_convert_fusion.1
  371.4 39.2 %reduce-scatter.11.cloned.1.call-done = bf16[288,768]{1,0:T(8,128)(2,1)} async-done(((bf16[1152,768]{1,0:T(8,128)(2,1)}), bf16[288,768]{1,0:T(8,128)(2,1)}) %reduce-scatter.11.cloned.1.call-update) | async-done | bytes 442384 | tf_op jit(solution)/shard_map/reduce_scatter | solution.py:227
  410.7 67.9 %reduce-scatter.9.cloned.1.call-done = bf16[192,2304]{1,0:T(8,128)(2,1)} async-done(((bf16[768,2304]{1,0:T(8,128)(2,1)}), bf16[192,2304]{1,0:T(8,128)(2,1)}) %reduce-scatter.9.cloned.1.call-update) | async-done | bytes 884752 | tf_op jit(solution)/shard_map/reduce_scatter | solution.py:224
  478.6 69.0 %reduce-scatter.5.cloned.1.call-done = bf16[192,2304]{1,0:T(8,128)(2,1)} async-done(((bf16[768,2304]{1,0:T(8,128)(2,1)}), bf16[192,2304]{1,0:T(8,128)(2,1)}) %reduce-scatter.5.cloned.1.call-update) | async-done | bytes 884752 | tf_op jit(solution)/shard_map/reduce_scatter | solution.py:218
  548.7 3.5 fusion.47
  552.6 10.7 %all-reduce.6 = (bf16[768]{0:T(1024)(128)(2,1)S(1)}, bf16[768]{0:T(1024)(128)(2,1)S(1)}) all-reduce(bf16[768]{0:T(1024)(128)(2,1)S(1)} %get-tuple-element.10, bf16[768]{0:T(1024)(128)(2,1)S(1)} %copy-done.43), channel_id=7, replica_groups=mesh['dp'=4,'ctx'=8] {'dp'}, use_global_device_ids=true, to_apply=%region_20.21.clone | all-reduce | flops 1536 | bytes 6144
  563.5 12.1 %all-reduce.4 = (bf16[192]{0:T(256)(128)(2,1)S(1)}, bf16[192]{0:T(256)(128)(2,1)S(1)}) all-reduce(bf16[192]{0:T(256)(128)(2,1)S(1)} %dynamic-slice.3, bf16[192]{0:T(256)(128)(2,1)S(1)} %dynamic-slice.5), channel_id=1, replica_groups=mesh['dp'=4,'ctx'=8] {'ctx'}, use_global_device_ids=true, to_apply=%region_21.22 | all-reduce | flops 384 | bytes 1536 | tf_op jit(solution)/shard_map/psum | solution.py:242
  577.7 39.2 %all-reduce.10.cloned.1.call-done = (bf16[192,2304]{1,0:T(8,128)(2,1)}, bf16[192,768]{1,0:T(8,128)(2,1)}, bf16[192,2304]{1,0:T(8,128)(2,1)}, bf16[288,768]{1,0:T(8,128)(2,1)}) async-done(((bf16[192,2304]{1,0:T(8,128)(2,1)}, bf16[192,768]{1,0:T(8,128)(2,1)}, bf16[192,2304]{1,0:T(8,128)(2,1)}, bf16[288,768]{1,0:T(8,128)(2,1)}), (bf16[192,2304]{1,0:T(8,128)(2,1)}, bf16[192,768]{1,0:T(8,128)(2,1)}, ...) | async-done | bytes 2506768 | tf_op jit(solution)/shard_map/psum | solution.py:238
  616.9 2.6 convert_element_type.150
  619.5 1.8 convert_element_type.152
  621.3 1.3 convert_element_type.154
  (178 shorter events, 22.5 us)
Async XLA Ops:
  7.2 75.2 %all-gather.10.cloned.1.call-start = ((), (), s32[]{:S(2)}) async-start(), calls=%async_computation.4 | async-start | bytes 4423680 | tf_op jit(solution)/shard_map/all_gather | solution.py:66
  7.9 106.1 %all-gather.14.cloned.1.call-start = ((), (), s32[]{:S(2)}) async-start(), calls=%async_computation.6 | async-start | bytes 1769472 | tf_op jit(solution)/shard_map/all_gather | solution.py:90
  26.1 89.7 %copy-start.22 = (f32[128,64]{0,1:T(8,128)}, f32[128,64]{0,1:T(8,128)S(1)}, u32[]{:S(2)}) copy-start(f32[128,64]{0,1:T(8,128)S(1)} %get-tuple-element.49) | copy-start | bytes 98308
  27.3 57.9 %copy-start.34 = (f32[128]{0:T(128)}, f32[128]{0:T(128)S(1)}, u32[]{:S(2)}) copy-start(f32[128]{0:T(128)S(1)} %broadcast_multiply_fusion.6) | copy-start | bytes 1540
  28.4 56.8 %copy-start.47 = (f32[128]{0:T(128)}, f32[128]{0:T(128)S(1)}, u32[]{:S(2)}) copy-start(f32[128]{0:T(128)S(1)} %fusion.46) | copy-start | bytes 1540
  28.5 56.8 %copy-start.36 = (f32[128]{0:T(128)}, f32[128]{0:T(128)S(1)}, u32[]{:S(2)}) copy-start(f32[128]{0:T(128)S(1)} %fusion.62) | copy-start | bytes 1540
  85.4 4.1 copy-start.4
  85.7 6.4 %copy-start.6 = (f32[128,12,64]{0,2,1:T(8,128)}, f32[128,12,64]{0,2,1:T(8,128)S(1)}, u32[]{:S(2)}) copy-start(f32[128,12,64]{0,2,1:T(8,128)S(1)} %get-tuple-element.45) | copy-start | bytes 1179652
  85.7 6.4 %copy-start.44 = (s32[1,128]{1,0:T(1,128)S(1)}, s32[1,128]{1,0:T(1,128)}, u32[]{:S(2)}) copy-start(s32[1,128]{1,0:T(1,128)} %param.10) | copy-start | bytes 1540
  89.6 52.1 %all-gather.12.cloned.1.call-start = ((), (), s32[]{:S(2)}) async-start(), calls=%async_computation.5 | async-start | bytes 1769472 | tf_op jit(solution)/shard_map/all_gather | solution.py:91
  90.4 83.2 %all-gather.16.cloned.1.call-start = ((), (), s32[]{:S(2)}) async-start(), calls=%async_computation.7 | async-start | bytes 1474560 | tf_op jit(solution)/shard_map/all_gather | solution.py:67
  90.9 153.2 %all-gather.18.cloned.1.call-start = ((), (), s32[]{:S(2)}) async-start(), calls=%async_computation.8 | async-start | bytes 4423680 | tf_op jit(solution)/shard_map/all_gather | solution.py:68
  91.5 192.9 %all-gather.20.cloned.1.call-start = ((), (), s32[]{:S(2)}) async-start(), calls=%async_computation.9 | async-start | bytes 2211840 | tf_op jit(solution)/shard_map/all_gather | solution.py:69
  92.1 219.4 %all-gather.22.cloned.1.call-start = ((), (), s32[]{:S(2)}) async-start(), calls=%async_computation.10 | async-start | bytes 1769472 | tf_op jit(solution)/shard_map/all_gather | solution.py:178
  100.9 16.1 %copy-start.31 = (s32[1,1024]{1,0:T(1,128)}, s32[1,1024]{1,0:T(1,128)S(1)}, u32[]{:S(2)}) copy-start(s32[1,1024]{1,0:T(1,128)S(1)} %all-gather) | copy-start | bytes 12292
  101.0 43.2 %copy-start.17 = (pred[128,1024]{1,0:T(8,128)(4,1)}, pred[128,1024]{1,0:T(8,128)(4,1)S(1)}, u32[]{:S(2)}) copy-start(pred[128,1024]{1,0:T(8,128)(4,1)S(1)} %broadcast_compare_fusion.1) | copy-start | bytes 393220
  101.1 239.2 %all-gather.24.cloned.1.call-start = ((), (), s32[]{:S(2)}) async-start(), calls=%async_computation.11 | async-start | bytes 1769472 | tf_op jit(solution)/shard_map/all_gather | solution.py:179
  121.7 28.3 %copy-start.32 = (f32[12,128]{1,0:T(8,128)}, f32[12,128]{1,0:T(8,128)S(1)}, u32[]{:S(2)}) copy-start(f32[12,128]{1,0:T(8,128)S(1)} %fusion.1) | copy-start | bytes 18436
  144.2 29.3 %copy-start.2 = (bf16[1,128,768]{2,1,0:T(8,128)(2,1)S(1)}, bf16[1,128,768]{2,1,0:T(8,128)(2,1)}, u32[]{:S(2)}) copy-start(bf16[1,128,768]{2,1,0:T(8,128)(2,1)} %param.9) | copy-start | bytes 589828
  150.0 26.0 %copy-start.21 = (bf16[128,12,64]{0,2,1:T(8,128)(2,1)}, bf16[128,12,64]{0,2,1:T(8,128)(2,1)S(1)}, u32[]{:S(2)}) copy-start(bf16[128,12,64]{0,2,1:T(8,128)(2,1)S(1)} %get-tuple-element.54) | copy-start | bytes 589828
  175.2 109.2 %copy-start.14 = (bf16[1,128,768]{2,1,0:T(8,128)(2,1)S(1)}, bf16[1,128,768]{2,1,0:T(8,128)(2,1)}, u32[]{:S(2)}) copy-start(bf16[1,128,768]{2,1,0:T(8,128)(2,1)} %param.17) | copy-start | bytes 589828
  284.5 4.2 copy-start.1
  284.5 4.2 copy-start.39
  284.5 4.2 copy-start.41
  287.8 2.8 copy-start.19
  290.6 4.4 copy-start.10
  292.3 4.7 copy-start.9
  292.3 79.2 %reduce-scatter.7.cloned.1.call-start = ((), (), s32[]{:S(2)}) async-start(), calls=%async_computation.13 | async-start | bytes 1474560 | tf_op jit(solution)/shard_map/reduce_scatter | solution.py:221
  294.9 115.8 %reduce-scatter.11.cloned.1.call-start = ((), (), s32[]{:S(2)}) async-start(), calls=%async_computation.15 | async-start | bytes 2211840 | tf_op jit(solution)/shard_map/reduce_scatter | solution.py:227
  296.9 5.7 copy-start.12
  296.9 181.7 %reduce-scatter.9.cloned.1.call-start = ((), (), s32[]{:S(2)}) async-start(), calls=%async_computation.14 | async-start | bytes 4423680 | tf_op jit(solution)/shard_map/reduce_scatter | solution.py:224
  300.9 34.1 %copy-start.5 = (f32[128,768]{0,1:T(8,128)S(1)}, f32[128,768]{0,1:T(8,128)}, u32[]{:S(2)}) copy-start(f32[128,768]{0,1:T(8,128)} %copy-done.4) | copy-start | bytes 1179652
  300.9 34.1 %copy-start.7 = (f32[128,12,64]{0,2,1:T(8,128)S(1)}, f32[128,12,64]{0,2,1:T(8,128)}, u32[]{:S(2)}) copy-start(f32[128,12,64]{0,2,1:T(8,128)} %copy-done.6) | copy-start | bytes 1179652
  300.9 246.6 %reduce-scatter.5.cloned.1.call-start = ((), (), s32[]{:S(2)}) async-start(), calls=%async_computation.12 | async-start | bytes 4423680 | tf_op jit(solution)/shard_map/reduce_scatter | solution.py:218
  314.8 10.1 %copy-start.33 = (f32[12,128]{1,0:T(8,128)}, f32[12,128]{1,0:T(8,128)S(1)}, u32[]{:S(2)}) copy-start(f32[12,128]{1,0:T(8,128)S(1)} %log_add_fusion) | copy-start | bytes 18436
  340.2 2.7 copy-start.30
  343.0 9.0 %copy-start.18 = (pred[128,1024]{1,0:T(8,128)(4,1)S(1)}, pred[128,1024]{1,0:T(8,128)(4,1)}, u32[]{:S(2)}) copy-start(pred[128,1024]{1,0:T(8,128)(4,1)} %copy-done.17) | copy-start | bytes 393220
  361.6 5.7 copy-start.35
  361.6 5.7 copy-start.37
  370.3 177.3 %copy-start.11 = (bf16[128,1152]{1,0:T(8,128)(2,1)S(1)}, bf16[128,1152]{1,0:T(8,128)(2,1)}, u32[]{:S(2)}) copy-start(bf16[128,1152]{1,0:T(8,128)(2,1)} %get-tuple-element.27) | copy-start | bytes 884740
  370.3 177.3 %copy-start.13 = (bf16[1152,768]{1,0:T(8,128)(2,1)S(1)}, bf16[1152,768]{1,0:T(8,128)(2,1)}, u32[]{:S(2)}) copy-start(bf16[1152,768]{1,0:T(8,128)(2,1)} %all-gather.20.cloned.1.call-done) | copy-start | bytes 5308420
  370.3 246.5 %all-reduce.10.cloned.1.call-start = ((), (), s32[]{:S(2)}) async-start(), calls=%async_computation.16 | async-start | bytes 5013504 | tf_op jit(solution)/shard_map/psum | solution.py:238
  548.7 3.5 copy-start.48
  548.7 3.8 copy-start.43
  548.7 28.0 %copy-start.15 = (bf16[1,128,768]{2,1,0:T(8,128)(2,1)S(1)}, bf16[1,128,768]{2,1,0:T(8,128)(2,1)}, u32[]{:S(2)}) copy-start(bf16[1,128,768]{2,1,0:T(8,128)(2,1)} %param.17) | copy-start | bytes 589828
  548.7 28.0 %copy-start.46 = (f32[128]{0:T(128)S(1)}, f32[128]{0:T(128)}, u32[]{:S(2)}) copy-start(f32[128]{0:T(128)} %copy-done.45) | copy-start | bytes 1540
  616.9 4.4 copy-start.20
  616.9 5.7 copy-start.23
  (16 other events, 32.4 us)
Sparse Core Ops, SparseCore 0:
  9.6 72.7 all-gather.9
  89.7 24.2 all-gather.13
  115.9 25.6 all-gather.11
  143.0 30.4 all-gather.15
  174.9 69.0 all-gather.17
  245.5 38.8 all-gather.19
  286.9 24.5 all-gather.21
  313.4 25.8 all-gather.23
  341.6 29.1 reduce-scatter.6
  373.6 37.0 reduce-scatter.10
  413.1 65.4 reduce-scatter.8
  480.9 66.6 reduce-scatter.4
  551.7 65.0 all-reduce.9
where the time goes:
time: 631 us; the launch traced here: 630 us
  waiting for transfers between devices  441 us (70%)
  blocking collectives  64.3 us (10%)
  matrix products  62.8 us (10%)
  other arithmetic  24.1 us (4%)
  local copies, waits for them, and re-layouts  21.3 us (3%)
  between operations  16 us (3%)
    reduce_scatter x1, waiting for transfers between devices, local(): lax.psum_scatter(local_grads[0].astype(jnp.bfloat16), 'dp', scatter_dimen...  69 us
    all_gather x1, waiting for transfers between devices, local(): lax.all_gather(shards[2], 'dp', axis=0, tiled=True)  68.1 us
    reduce_scatter x1, waiting for transfers between devices, local(): lax.psum_scatter(local_grads[2].astype(jnp.bfloat16), 'dp', scatter_dimen...  67.9 us
    all_gather x1, waiting for transfers between devices, local(): lax.all_gather(shards[0], 'dp', axis=0, tiled=True)  53.9 us
    reduce_scatter x1, waiting for transfers between devices, local(): lax.psum_scatter(local_grads[3].astype(jnp.bfloat16), 'dp', scatter_dimen...  39.2 us
    psum x1, waiting for transfers between devices, local(): lax.psum(shares[0].astype(jnp.bfloat16), 'ctx').astype(jnp.float32)  39.2 us
    all_gather x1, waiting for transfers between devices, local(): lax.all_gather(shards[3], 'dp', axis=0, tiled=True)  37.7 us
    unnamed x2, blocking collectives  24.3 us
  transfers between devices with their start and end apart: 13, of which 11 were waited for; matrix products, arithmetic and copies ran while one was open for 14% of the time, Pallas kernels for 0%

commit v1 on v0

--- a/solution.py
+++ b/solution.py
@@ -87,8 +87,11 @@
     key_flat = own_keys.reshape(local_rows, model_width)
     query_flat = queries.reshape(local_rows, model_width)
     highest = jnp.full((head_count, local_rows), NEGATIVE, jnp.float32)
-    block_keys = lax.all_gather(key_flat, "ctx", axis=0, tiled=True)
-    block_values = lax.all_gather(value_flat, "ctx", axis=0, tiled=True)
+    block_keys, block_values = jnp.split(
+        lax.all_gather(jnp.concatenate([key_flat, value_flat], axis=1), "ctx", axis=0, tiled=True),
+        [key_flat.shape[1]],
+        axis=1,
+    )
     block_ids = lax.all_gather(own_ids, "ctx", axis=0, tiled=True)
     piece_rows = block_keys.shape[0]
     scores = (

time: 631 us -> 668 us (1.059)
  waiting for transfers between devices: 441 us -> 470 us
    all_gather x0 -> x1, waiting for transfers between devices: none -> 17.4 us  [local(): lax.all_gather(jnp.concatenate([key_flat, value_flat], axis=1), 'ctx', ax...]
    all_gather x1, waiting for transfers between devices: 12.9 us -> 25 us  [local(): block_keys = lax.all_gather(key_flat, 'ctx', axis=0, tiled=True)]
    all_gather x1, waiting for transfers between devices: 23.5 us -> 13.6 us  [local(): lax.all_gather(shards[1], 'dp', axis=0, tiled=True)]
  transfers between devices with their start and end apart: 13 -> 14, of which waited for: 11 -> 12; matrix products, arithmetic and copies ran while one was open for 14% -> 15% of each run, Pallas kernels for 0% -> 0%
where the time goes in v1:
time: 668 us; the launch traced here: 667 us
  waiting for transfers between devices  470 us (70%)
  matrix products  64.9 us (10%)
  blocking collectives  62.3 us (9%)
  other arithmetic  28.6 us (4%)
  local copies, waits for them, and re-layouts  23.9 us (4%)
  between operations  16 us (2%)
    reduce_scatter x1, waiting for transfers between devices, local(): lax.psum_scatter(local_grads[0].astype(jnp.bfloat16), 'dp', scatter_dimen...  69.1 us
    all_gather x1, waiting for transfers between devices, local(): lax.all_gather(shards[2], 'dp', axis=0, tiled=True)  68.6 us
    reduce_scatter x1, waiting for transfers between devices, local(): lax.psum_scatter(local_grads[2].astype(jnp.bfloat16), 'dp', scatter_dimen...  67.8 us
    all_gather x1, waiting for transfers between devices, local(): lax.all_gather(shards[0], 'dp', axis=0, tiled=True)  53.3 us
    reduce_scatter x1, waiting for transfers between devices, local(): lax.psum_scatter(local_grads[3].astype(jnp.bfloat16), 'dp', scatter_dimen...  39.8 us
    psum x1, waiting for transfers between devices, local(): lax.psum(shares[0].astype(jnp.bfloat16), 'ctx').astype(jnp.float32)  37.7 us
    all_gather x1, waiting for transfers between devices, local(): lax.all_gather(shards[3], 'dp', axis=0, tiled=True)  37.7 us
    all_gather x1, waiting for transfers between devices, local(): block_values = lax.all_gather(value_flat, 'ctx', axis=0, tiled=True)  25.9 us
  transfers between devices with their start and end apart: 14, of which 12 were waited for; matrix products, arithmetic and copies ran while one was open for 15% of the time, Pallas kernels for 0%

profile of v1, /device:TPU:0, one launch (start us, length us, event | category | flops | bytes accessed | tf_op | source)
XLA Modules:
  0.0 666.8 jit_solution(9748130313936963109)
XLA Ops:
  8.0 1.3 fusion.87
  11.6 13.6 %all-reduce.7 = (bf16[768]{0:T(1024)(128)(2,1)S(1)}, bf16[768]{0:T(1024)(128)(2,1)S(1)}) all-reduce(bf16[768]{0:T(1024)(128)(2,1)S(1)} %dynamic-update-slice, bf16[768]{0:T(1024)(128)(2,1)S(1)} %dynamic-update-slice.1), channel_id=1, replica_groups=mesh['dp'=4,'ctx'=8] {'dp'}, use_global_device_ids=true, to_apply=%add | all-reduce | flops 1536 | bytes 6144
  29.0 53.3 %all-gather.11.cloned.1.call-done = bf16[768,2304]{1,0:T(8,128)(2,1)} async-done(((bf16[192,2304]{1,0:T(8,128)(2,1)}), bf16[768,2304]{1,0:T(8,128)(2,1)}) %all-gather.11.cloned.1.call-update) | async-done | bytes 3538960 | tf_op jit(solution)/shard_map/all_gather | solution.py:66
  82.3 2.8 fusion.77
  85.7 1.7 add_convert_fusion.3
  89.6 1.8 add_convert_fusion.2
  95.5 8.7 %all-gather = s32[1,1024]{1,0:T(1,128)S(1)} all-gather(s32[1,128]{1,0:T(1,128)S(1)} %copy-done.45), channel_id=2, replica_groups=mesh['dp'=4,'ctx'=8] {'ctx'}, dimensions={1}, use_global_device_ids=true | all-gather | bytes 4608 | tf_op jit(solution)/shard_map/all_gather | solution.py:95
  105.9 17.4 %all-gather.13.cloned.1.call-done = bf16[1024,1536]{1,0:T(8,128)(2,1)} async-done(((bf16[128,1536]{1,0:T(8,128)(2,1)}), bf16[1024,1536]{1,0:T(8,128)(2,1)}) %all-gather.13.cloned.1.call-update) | async-done | bytes 3145744 | tf_op jit(solution)/shard_map/all_gather | solution.py:91
  123.3 3.2 fusion.83
  126.5 1.7 copy.52
  128.2 4.9 fusion
  134.5 4.3 fusion.2
  139.2 2.5 fusion.88
  141.7 13.6 %all-gather.15.cloned.1.call-done = bf16[768,768]{1,0:T(8,128)(2,1)} async-done(((bf16[192,768]{1,0:T(8,128)(2,1)}), bf16[768,768]{1,0:T(8,128)(2,1)}) %all-gather.15.cloned.1.call-update) | async-done | bytes 1179664 | tf_op jit(solution)/shard_map/all_gather | solution.py:67
  155.3 1.7 fusion.89
  157.3 68.6 %all-gather.17.cloned.1.call-done = bf16[768,2304]{1,0:T(8,128)(2,1)} async-done(((bf16[192,2304]{1,0:T(8,128)(2,1)}), bf16[768,2304]{1,0:T(8,128)(2,1)}) %all-gather.17.cloned.1.call-update) | async-done | bytes 3538960 | tf_op jit(solution)/shard_map/all_gather | solution.py:68
  225.9 2.7 fusion.80
  228.6 37.7 %all-gather.19.cloned.1.call-done = bf16[1152,768]{1,0:T(8,128)(2,1)} async-done(((bf16[288,768]{1,0:T(8,128)(2,1)}), bf16[1152,768]{1,0:T(8,128)(2,1)}) %all-gather.19.cloned.1.call-update) | async-done | bytes 1769488 | tf_op jit(solution)/shard_map/all_gather | solution.py:69
  266.3 3.3 add_convert_fusion
  269.8 1.9 multiply_reduce_fusion
  274.1 1.5 convolution_convert_fusion.3
  275.7 1.9 convolution_convert_fusion.2
  277.7 3.0 convolution_convert_fusion
  282.6 10.6 %all-gather.25.cloned.1.call-done = bf16[1024,768]{1,0:T(8,128)(2,1)} async-done(((bf16[128,768]{1,0:T(8,128)(2,1)}), bf16[1024,768]{1,0:T(8,128)(2,1)}) %all-gather.25.cloned.1.call-update) | async-done | bytes 1572880 | tf_op jit(solution)/shard_map/all_gather | solution.py:181
  293.2 2.6 copy.58
  295.8 25.0 %all-gather.21.cloned.1.call-done = bf16[1024,768]{1,0:T(8,128)(2,1)} async-done(((bf16[128,768]{1,0:T(8,128)(2,1)}), bf16[1024,768]{1,0:T(8,128)(2,1)}) %all-gather.21.cloned.1.call-update) | async-done | bytes 1572880 | tf_op jit(solution)/shard_map/all_gather | solution.py:160
  320.8 1.7 copy.53
  322.5 25.9 %all-gather.23.cloned.1.call-done = bf16[1024,768]{1,0:T(8,128)(2,1)} async-done(((bf16[128,768]{1,0:T(8,128)(2,1)}), bf16[1024,768]{1,0:T(8,128)(2,1)}) %all-gather.23.cloned.1.call-update) | async-done | bytes 1572880 | tf_op jit(solution)/shard_map/all_gather | solution.py:161
  348.4 2.7 copy.55
  351.1 3.7 fusion.90
  354.8 3.8 fusion.54
  359.5 9.0 %all_gather.61 = f32[12,1024]{1,0:T(8,128)S(1)} all-gather(f32[12,128]{1,0:T(8,128)S(1)} %log_add_fusion), channel_id=1, replica_groups=mesh['dp'=4,'ctx'=8] {'ctx'}, dimensions={1}, use_global_device_ids=true | all-gather | bytes 55296 | tf_op jit(solution)/shard_map/all_gather | solution.py:156
  369.6 8.3 %all_gather.63 = f32[12,1024]{1,0:T(8,128)S(1)} all-gather(f32[12,128]{1,0:T(8,128)S(1)} %bitcast.137), channel_id=1, replica_groups=mesh['dp'=4,'ctx'=8] {'ctx'}, dimensions={1}, use_global_device_ids=true | all-gather | bytes 55296 | tf_op jit(solution)/shard_map/all_gather | solution.py:157
  377.8 2.6 copy.59
  380.4 9.0 %fusion.18 = f32[128,12,64]{0,2,1:T(8,128)} fusion(bf16[1024,12,64]{0,2,1:T(8,128)(2,1)} %bitcast.110, f32[12,1024,128]{2,1,0:T(8,128)} %fusion.54, f32[12,1024]{1,0:T(8,128)S(1)} %all_gather.63, f32[12,1024]{1,0:T(8,128)S(1)} %all_gather.61, pred[1024,128]{1,0:T(8,128)(4,1)S(1)} %copy-done.29, bf16[1024,12,64]{0,2,1:T(8,128)(2,1)} %bitcast.117, ...), kind=kOutput, calls=%fused_computation.23 | convolution fusion | flops 412090368 | bytes 10256384 | tf_op jit(solution)/shard_map/hqk,qhe->khe/dot_general | solution.py:202
  389.4 7.1 %broadcast_multiply_fusion.1 = (f32[128,12,64]{0,2,1:T(8,128)}, f32[128,12,64]{0,2,1:T(8,128)S(1)}, f32[128,12,64]{0,2,1:T(8,128)}) fusion(f32[128,64]{0,1:T(8,128)} %get-tuple-element.50, f32[128,12,64]{0,2,1:T(8,128)} %fusion.18, bf16[1024,12,64]{0,2,1:T(8,128)(2,1)S(1)} %bitcast.109, f32[12,128,1024]{2,1,0:T(8,128)} %fusion.90, ...), kind=kOutput, calls=%fused_computation.103 | convolution fusion | flops 412286976 | bytes 11382784 | tf_op jit(solution)/shard_map/hqk,khe->qhe/dot_general | solution.py:178
  399.0 5.0 fusion.24
  404.1 3.0 convolution_convert_fusion.1
  407.9 39.8 %reduce-scatter.11.cloned.1.call-done = bf16[288,768]{1,0:T(8,128)(2,1)} async-done(((bf16[1152,768]{1,0:T(8,128)(2,1)}), bf16[288,768]{1,0:T(8,128)(2,1)}) %reduce-scatter.11.cloned.1.call-update) | async-done | bytes 442384 | tf_op jit(solution)/shard_map/reduce_scatter | solution.py:230
  447.6 67.8 %reduce-scatter.9.cloned.1.call-done = bf16[192,2304]{1,0:T(8,128)(2,1)} async-done(((bf16[768,2304]{1,0:T(8,128)(2,1)}), bf16[192,2304]{1,0:T(8,128)(2,1)}) %reduce-scatter.9.cloned.1.call-update) | async-done | bytes 884752 | tf_op jit(solution)/shard_map/reduce_scatter | solution.py:227
  515.4 69.1 %reduce-scatter.5.cloned.1.call-done = bf16[192,2304]{1,0:T(8,128)(2,1)} async-done(((bf16[768,2304]{1,0:T(8,128)(2,1)}), bf16[192,2304]{1,0:T(8,128)(2,1)}) %reduce-scatter.5.cloned.1.call-update) | async-done | bytes 884752 | tf_op jit(solution)/shard_map/reduce_scatter | solution.py:221
  584.5 2.6 fusion.27
  587.1 3.4 fusion.48
  590.9 10.7 %all-reduce.6 = (bf16[768]{0:T(1024)(128)(2,1)S(1)}, bf16[768]{0:T(1024)(128)(2,1)S(1)}) all-reduce(bf16[768]{0:T(1024)(128)(2,1)S(1)} %get-tuple-element.10, bf16[768]{0:T(1024)(128)(2,1)S(1)} %copy-done.44), channel_id=7, replica_groups=mesh['dp'=4,'ctx'=8] {'dp'}, use_global_device_ids=true, to_apply=%region_20.21.clone | all-reduce | flops 1536 | bytes 6144
  601.7 12.0 %all-reduce.4 = (bf16[192]{0:T(256)(128)(2,1)S(1)}, bf16[192]{0:T(256)(128)(2,1)S(1)}) all-reduce(bf16[192]{0:T(256)(128)(2,1)S(1)} %dynamic-slice.3, bf16[192]{0:T(256)(128)(2,1)S(1)} %dynamic-slice.5), channel_id=1, replica_groups=mesh['dp'=4,'ctx'=8] {'ctx'}, use_global_device_ids=true, to_apply=%region_21.22 | all-reduce | flops 384 | bytes 1536 | tf_op jit(solution)/shard_map/psum | solution.py:245
  615.8 37.7 %all-reduce.10.cloned.1.call-done = (bf16[192,2304]{1,0:T(8,128)(2,1)}, bf16[192,768]{1,0:T(8,128)(2,1)}, bf16[192,2304]{1,0:T(8,128)(2,1)}, bf16[288,768]{1,0:T(8,128)(2,1)}) async-done(((bf16[192,2304]{1,0:T(8,128)(2,1)}, bf16[192,768]{1,0:T(8,128)(2,1)}, bf16[192,2304]{1,0:T(8,128)(2,1)}, bf16[288,768]{1,0:T(8,128)(2,1)}), (bf16[192,2304]{1,0:T(8,128)(2,1)}, bf16[192,768]{1,0:T(8,128)(2,1)}, ...) | async-done | bytes 2506768 | tf_op jit(solution)/shard_map/psum | solution.py:241
  653.6 2.6 convert_element_type.150
  656.2 1.8 convert_element_type.152
  (186 shorter events, 30.4 us)
Async XLA Ops:
  7.2 75.2 %all-gather.11.cloned.1.call-start = ((), (), s32[]{:S(2)}) async-start(), calls=%async_computation.4 | async-start | bytes 4423680 | tf_op jit(solution)/shard_map/all_gather | solution.py:66
  7.9 115.4 %all-gather.13.cloned.1.call-start = ((), (), s32[]{:S(2)}) async-start(), calls=%async_computation.5 | async-start | bytes 3538944 | tf_op jit(solution)/shard_map/all_gather | solution.py:91
  27.9 54.5 %copy-start.36 = (f32[128]{0:T(128)}, f32[128]{0:T(128)S(1)}, u32[]{:S(2)}) copy-start(f32[128]{0:T(128)S(1)} %broadcast_multiply_fusion.6) | copy-start | bytes 1540
  29.0 56.2 %copy-start.49 = (f32[128]{0:T(128)}, f32[128]{0:T(128)S(1)}, u32[]{:S(2)}) copy-start(f32[128]{0:T(128)S(1)} %fusion.47) | copy-start | bytes 1540
  29.0 53.3 %copy-start.38 = (f32[128]{0:T(128)}, f32[128]{0:T(128)S(1)}, u32[]{:S(2)}) copy-start(f32[128]{0:T(128)S(1)} %fusion.61) | copy-start | bytes 1540
  85.3 6.1 copy-start.7
  87.4 6.2 copy-start.5
  88.7 6.8 %copy-start.45 = (s32[1,128]{1,0:T(1,128)S(1)}, s32[1,128]{1,0:T(1,128)}, u32[]{:S(2)}) copy-start(s32[1,128]{1,0:T(1,128)} %param.10) | copy-start | bytes 1540
  92.2 63.1 %all-gather.15.cloned.1.call-start = ((), (), s32[]{:S(2)}) async-start(), calls=%async_computation.6 | async-start | bytes 1474560 | tf_op jit(solution)/shard_map/all_gather | solution.py:67
  93.0 132.9 %all-gather.17.cloned.1.call-start = ((), (), s32[]{:S(2)}) async-start(), calls=%async_computation.7 | async-start | bytes 4423680 | tf_op jit(solution)/shard_map/all_gather | solution.py:68
  93.6 172.7 %all-gather.19.cloned.1.call-start = ((), (), s32[]{:S(2)}) async-start(), calls=%async_computation.8 | async-start | bytes 2211840 | tf_op jit(solution)/shard_map/all_gather | solution.py:69
  94.1 199.0 %all-gather.25.cloned.1.call-start = ((), (), s32[]{:S(2)}) async-start(), calls=%async_computation.11 | async-start | bytes 1769472 | tf_op jit(solution)/shard_map/all_gather | solution.py:181
  94.7 226.1 %all-gather.21.cloned.1.call-start = ((), (), s32[]{:S(2)}) async-start(), calls=%async_computation.9 | async-start | bytes 1769472 | tf_op jit(solution)/shard_map/all_gather | solution.py:160
  95.5 252.9 %all-gather.23.cloned.1.call-start = ((), (), s32[]{:S(2)}) async-start(), calls=%async_computation.10 | async-start | bytes 1769472 | tf_op jit(solution)/shard_map/all_gather | solution.py:161
  105.7 272.2 %all-gather.27.cloned.1.call-start = ((), (), s32[]{:S(2)}) async-start(), calls=%async_computation.12 | async-start | bytes 1769472 | tf_op jit(solution)/shard_map/all_gather | solution.py:182
  134.5 4.7 copy-start
  134.5 4.7 copy-start.17
  134.5 4.7 copy-start.35
  139.2 16.2 %copy-start.2 = (bf16[1,128,768]{2,1,0:T(8,128)(2,1)S(1)}, bf16[1,128,768]{2,1,0:T(8,128)(2,1)}, u32[]{:S(2)}) copy-start(bf16[1,128,768]{2,1,0:T(8,128)(2,1)} %param.9) | copy-start | bytes 589828
  141.7 15.6 %copy-start.22 = (bf16[128,12,64]{0,2,1:T(8,128)(2,1)}, bf16[128,12,64]{0,2,1:T(8,128)(2,1)S(1)}, u32[]{:S(2)}) copy-start(bf16[128,12,64]{0,2,1:T(8,128)(2,1)S(1)} %get-tuple-element.57) | copy-start | bytes 589828
  157.1 109.2 %copy-start.13 = (bf16[1,128,768]{2,1,0:T(8,128)(2,1)S(1)}, bf16[1,128,768]{2,1,0:T(8,128)(2,1)}, u32[]{:S(2)}) copy-start(bf16[1,128,768]{2,1,0:T(8,128)(2,1)} %param.17) | copy-start | bytes 589828
  157.1 112.7 %copy-start.40 = (f32[128]{0:T(128)}, f32[128]{0:T(128)S(1)}, u32[]{:S(2)}) copy-start(f32[128]{0:T(128)S(1)} %broadcast_multiply_fusion.5) | copy-start | bytes 1540
  157.3 112.5 %copy-start.42 = (f32[128]{0:T(128)}, f32[128]{0:T(128)S(1)}, u32[]{:S(2)}) copy-start(f32[128]{0:T(128)S(1)} %fusion.62) | copy-start | bytes 1540
  269.8 5.9 copy-start.9
  269.8 4.3 copy-start.23
  274.0 133.8 %reduce-scatter.7.cloned.1.call-start = ((), (), s32[]{:S(2)}) async-start(), calls=%async_computation.14 | async-start | bytes 1474560 | tf_op jit(solution)/shard_map/reduce_scatter | solution.py:224
  275.6 172.0 %reduce-scatter.11.cloned.1.call-start = ((), (), s32[]{:S(2)}) async-start(), calls=%async_computation.16 | async-start | bytes 2211840 | tf_op jit(solution)/shard_map/reduce_scatter | solution.py:230
  277.6 4.2 copy-start.8
  277.6 237.8 %reduce-scatter.9.cloned.1.call-start = ((), (), s32[]{:S(2)}) async-start(), calls=%async_computation.15 | async-start | bytes 4423680 | tf_op jit(solution)/shard_map/reduce_scatter | solution.py:227
  280.6 303.8 %reduce-scatter.5.cloned.1.call-start = ((), (), s32[]{:S(2)}) async-start(), calls=%async_computation.13 | async-start | bytes 4423680 | tf_op jit(solution)/shard_map/reduce_scatter | solution.py:221
  295.8 55.3 %copy-start.15 = (bf16[128,12,64]{0,2,1:T(8,128)(2,1)S(1)}, bf16[128,12,64]{0,2,1:T(8,128)(2,1)}, u32[]{:S(2)}) copy-start(bf16[128,12,64]{0,2,1:T(8,128)(2,1)} %get-tuple-element.26) | copy-start | bytes 589828
  351.1 3.7 copy-start.3
  351.1 3.7 copy-start.6
  354.8 3.8 copy-start.12
  358.6 21.8 %copy-start.27 = (bf16[128,768]{0,1:T(8,128)(2,1)S(1)}, bf16[128,768]{0,1:T(8,128)(2,1)}, u32[]{:S(2)}) copy-start(bf16[128,768]{0,1:T(8,128)(2,1)} %copy.60) | copy-start | bytes 589828
  358.6 21.8 %copy-start.29 = (pred[1024,128]{1,0:T(8,128)(4,1)S(1)}, pred[1024,128]{1,0:T(8,128)(4,1)}, u32[]{:S(2)}) copy-start(pred[1024,128]{1,0:T(8,128)(4,1)} %broadcast_compare_fusion) | copy-start | bytes 393220
  368.5 20.9 %copy-start.30 = (f32[12,1024]{1,0:T(8,128)}, f32[12,1024]{1,0:T(8,128)S(1)}, u32[]{:S(2)}) copy-start(f32[12,1024]{1,0:T(8,128)S(1)} %all_gather.61) | copy-start | bytes 147460
  380.4 9.0 %copy-start.18 = (pred[128,1024]{1,0:T(8,128)(4,1)S(1)}, pred[128,1024]{1,0:T(8,128)(4,1)}, u32[]{:S(2)}) copy-start(pred[128,1024]{1,0:T(8,128)(4,1)} %broadcast_compare_fusion.1) | copy-start | bytes 393220
  389.4 8.4 %copy-start.28 = (f32[128,64]{0,1:T(8,128)S(1)}, f32[128,64]{0,1:T(8,128)}, u32[]{:S(2)}) copy-start(f32[128,64]{0,1:T(8,128)} %get-tuple-element.49) | copy-start | bytes 98308
  399.0 5.1 copy-start.37
  399.0 5.1 copy-start.39
  407.1 177.4 %copy-start.10 = (bf16[128,1152]{1,0:T(8,128)(2,1)S(1)}, bf16[128,1152]{1,0:T(8,128)(2,1)}, u32[]{:S(2)}) copy-start(bf16[128,1152]{1,0:T(8,128)(2,1)} %copy-done.9) | copy-start | bytes 884740
  407.1 246.5 %all-reduce.10.cloned.1.call-start = ((), (), s32[]{:S(2)}) async-start(), calls=%async_computation.17 | async-start | bytes 5013504 | tf_op jit(solution)/shard_map/psum | solution.py:241
  587.1 3.7 copy-start.44
  587.1 27.7 %copy-start.14 = (bf16[1,128,768]{2,1,0:T(8,128)(2,1)S(1)}, bf16[1,128,768]{2,1,0:T(8,128)(2,1)}, u32[]{:S(2)}) copy-start(bf16[1,128,768]{2,1,0:T(8,128)(2,1)} %param.17) | copy-start | bytes 589828
  587.1 27.7 %copy-start.48 = (f32[128]{0:T(128)S(1)}, f32[128]{0:T(128)}, u32[]{:S(2)}) copy-start(f32[128]{0:T(128)} %copy-done.47) | copy-start | bytes 1540
  653.6 4.4 copy-start.21
  653.6 5.7 copy-start.26
  (17 other events, 47.2 us)
Sparse Core Ops, SparseCore 0:
  9.6 72.7 all-gather.10
  92.3 30.8 all-gather.12
  124.9 30.4 all-gather.14
  156.8 69.0 all-gather.16
  227.3 38.8 all-gather.18
  268.6 24.5 all-gather.24
  295.1 25.6 all-gather.20
  322.7 25.6 all-gather.22
  350.3 25.8 all-gather.26
  378.3 29.1 reduce-scatter.6
  410.5 37.0 reduce-scatter.10
  449.9 65.4 reduce-scatter.8
  517.8 66.6 reduce-scatter.4
  588.5 65.0 all-reduce.9
